TPU v7x, 32 devices: a whole 2x2x4 slice. The times are simulated.
32 devices in a mesh: grp: 2 (over x), lon: 8 (over z, y), lat: 2 (over core).
Axes of the slice: x: 2, y: 2, z: 4, core: 2. Of those that a mesh axis runs over, the one named last changes fastest.
Arguments:
- cloud_state: float32 [4, 256, 128, 1024], P('grp', 'lon', 'lat'), parts along dimension 0, may hold values from -6 to 6
- counts: int32 [512, 128], P(('grp', 'lon'), 'lat'), parts along dimension 0, may hold values from 1 to 8, as said below
- courant: float32 [32], replicated, may hold values from 0.2 to 0.9
- truncation: int32 [96], replicated, may hold values from 0 to 94, as said below
Outputs:
- cloud_next: float32 [4, 256, 128, 1024], P('grp', 'lon', 'lat'), parts along dimension 0
There are 2 independent parts, one for each index of `grp`. A program takes and returns all parts, laid end to end along the dimension named above; an argument that names none is the same for every part. Nothing has to cross between parts.
Inputs may be any that keep to these rules, and one draw needn't show every extreme that they name: `counts`: columns come in busy regions of 4 to 8 substeps and calm ones of 1 or 2; column 0, 0 has 8. truncation[m] lies in m .. 85 for m <= 85, truncation[0] = 85, and truncation[m] = m - 1 (nothing kept) for m > 85.
All inputs are finite; a program needn't handle non-finite values.
Results may differ from a plain program's by a relative error of at most 0.0003.
Values sent between devices are 32-bit elements; how exact they have to be, the bound alone decides.
A program may use at most 64 MiB of HBM per device.

v0:
```python
import functools

import jax
import jax.numpy as jnp
import numpy as np
from jax import lax
from jax.experimental import pallas as pl
from jax.experimental.pallas import tpu as pltpu
from jax.sharding import PartitionSpec as P

NN = 96
COUPLE = 8.0
HIGHEST = lax.Precision.HIGHEST
MESH = pl.DeviceIdType.MESH


def wave_tables(total_lon, lon_devices, modes, peers, scale):
    per_peer = modes // peers
    lon_local = total_lon // lon_devices
    rows = np.zeros((peers, 2, 8, total_lon))
    back = np.zeros((peers, 2, 8, total_lon))
    lons = np.arange(total_lon)
    for peer in range(peers):
        for at in range(per_peer):
            mode = peer * per_peer + at
            angle = 2.0 * np.pi * ((lons * mode) % total_lon) / total_lon
            rows[peer, 0, at], rows[peer, 1, at] = np.cos(angle), np.sin(angle)
            back[peer, :, at] = rows[peer, :, at] * (1.0 if mode == 0 else 2.0)
    rows = rows.reshape(peers * 16, lon_devices, lon_local).transpose(1, 0, 2) * scale
    back = back.reshape(peers * 16, lon_devices, lon_local).transpose(1, 2, 0)
    return rows.astype(np.float32), back.astype(np.float32)


def latitude_rows(total_lat):
    latitude = -0.5 * np.pi + np.pi * (np.arange(total_lat) + 0.5) / total_lat
    cosine = np.cos(latitude)
    rows = np.stack([np.sin(latitude), np.pi * cosine / total_lat, np.log(cosine)])
    return np.repeat(rows[:, None, :], 8, axis=1).astype(np.float32)


def order_starts(modes, total_lat):
    ladder = np.arange(1, modes + 8)
    gains = np.concatenate([[0.0], np.cumsum(0.5 * np.log((2.0 * ladder + 1.0) / (2.0 * ladder)))])
    return np.repeat((0.5 * np.log(0.5) + gains)[:, None], total_lat, axis=1).astype(np.float32)


def spectral_kernel(
    lon_devices, lat_devices, modes, chunks,
    trunc_ref, state_ref, forward_ref, back_ref, lat_ref, start_ref, out_ref,
    theta, table, heat, forward, back, send1, recv1, send2, recv2,
    load_sem, table_sem, s1_sem, r1_sem, s2_sem, r2_sem,
):
    grp = lax.axis_index("grp")
    lon = lax.axis_index("lon")
    lat = lax.axis_index("lat")
    peers = lon_devices * lat_devices
    per_peer = modes // peers
    me = lon * lat_devices + lat
    lon_local, lat_local, cells = theta.shape
    rows = lon_local // chunks

    def theta_copy(chunk):
        span = pl.ds(chunk * rows, rows)
        return pltpu.make_async_copy(state_ref.at[0, span], theta.at[span], load_sem.at[chunk])

    for chunk in range(chunks):
        theta_copy(chunk).start()
    forward_copy = pltpu.make_async_copy(forward_ref.at[lon], forward, table_sem.at[0])
    back_copy = pltpu.make_async_copy(back_ref.at[lon], back, table_sem.at[1])
    forward_copy.start()
    back_copy.start()

    barrier = pltpu.get_barrier_semaphore()

    def place(offset):
        peer = lax.rem(me + offset, peers)
        return peer, (grp, peer // lat_devices, lax.rem(peer, lat_devices))

    def greet(offset, carry):
        _, device = place(offset)
        pl.semaphore_signal(barrier, inc=1, device_id=device, device_id_type=MESH)
        return carry

    lax.fori_loop(1, peers, greet, 0)

    total_lat = table.shape[1]
    sin_lat = lat_ref[0]
    weight = lat_ref[1]
    order_f = (me * per_peer + lax.broadcasted_iota(jnp.int32, (8, total_lat), 0)).astype(jnp.float32)
    start = jnp.concatenate(
        [start_ref[pl.ds(me * per_peer + at, 1), :] for at in range(8)], axis=0
    )
    diagonal = jnp.exp(start + order_f * lat_ref[2])
    zero = jnp.zeros((8, total_lat), jnp.float32)

    def rung(degree_f, carry):
        previous, earlier, inverse = carry
        higher = degree_f > order_f
        numerator = jnp.maximum(4.0 * degree_f * degree_f - 1.0, 1.0)
        denominator = jnp.where(higher, degree_f * degree_f - order_f * order_f, 1.0)
        factor = jnp.sqrt(numerator / denominator)
        back_factor = jnp.sqrt(denominator / numerator)
        raised = factor * (sin_lat * previous - inverse * earlier)
        current = jnp.where(degree_f == order_f, diagonal, jnp.where(higher, raised, 0.0))
        return current, previous, jnp.where(higher, back_factor, 0.0)

    def ladder(block, carry):
        for at in range(8):
            degree = block * 8 + at
            carry = rung(degree.astype(jnp.float32), carry)
            table[pl.ds(pl.multiple_of(degree * 8, 8), 8), :] = carry[0]
        return carry

    lax.fori_loop(0, NN // 8, ladder, (zero, zero, zero))

    ones = jnp.ones((8, 128), jnp.float32)
    for chunk in range(chunks):
        theta_copy(chunk).wait()

        def add_row(at, carry):
            row = chunk * rows + at
            total = theta[row, :, 0:128]
            for tile in range(1, cells // 128):
                total = total + theta[row, :, tile * 128:(tile + 1) * 128]
            heat[row] = lax.dot_general(
                ones, total, (((1,), (1,)), ((), ())),
                precision=HIGHEST, preferred_element_type=jnp.float32,
            )
            return carry

        lax.fori_loop(0, rows, add_row, 0)
    forward_copy.wait()
    back_copy.wait()
    heating = heat[:, 0, :]
    coefs = jnp.dot(forward[...], heating, precision=HIGHEST, preferred_element_type=jnp.float32)
    send1[...] = coefs.reshape(peers, 16, lat_local)
    pl.semaphore_wait(barrier, peers - 1)

    def first(offset):
        peer, device = place(offset)
        return pltpu.make_async_remote_copy(
            src_ref=send1.at[peer], dst_ref=recv1.at[me],
            send_sem=s1_sem.at[peer], recv_sem=r1_sem.at[me],
            device_id=device, device_id_type=MESH,
        )

    def first_arrival(offset):
        peer, device = place(offset)
        return pltpu.make_async_remote_copy(
            src_ref=send1.at[peer], dst_ref=recv1.at[peer],
            send_sem=s1_sem.at[peer], recv_sem=r1_sem.at[peer],
            device_id=device, device_id_type=MESH,
        )

    def second(offset):
        peer, device = place(offset)
        return pltpu.make_async_remote_copy(
            src_ref=send2.at[lax.rem(peer, lat_devices)], dst_ref=recv2.at[me],
            send_sem=s2_sem.at[peer], recv_sem=r2_sem.at[me],
            device_id=device, device_id_type=MESH,
        )

    def second_arrival(offset):
        peer, device = place(offset)
        return pltpu.make_async_remote_copy(
            src_ref=send2.at[lax.rem(peer, lat_devices)], dst_ref=recv2.at[peer],
            send_sem=s2_sem.at[peer], recv_sem=r2_sem.at[peer],
            device_id=device, device_id_type=MESH,
        )

    def for_peers(act):
        def step(offset, carry):
            act(offset)
            return carry
        lax.fori_loop(1, peers, step, 0)

    for_peers(lambda offset: first(offset).start())
    recv1[me] = send1[me]
    for_peers(lambda offset: first_arrival(offset).wait_recv())
    halves = []
    for half in range(lat_devices):
        total = recv1[half]
        for at in range(1, lon_devices):
            total = total + recv1[at * lat_devices + half]
        halves.append(total)
    whole = jnp.concatenate(halves, axis=1)
    weighted = whole * jnp.concatenate([weight, weight], axis=0)

    width = table.shape[0]
    spectrum = lax.dot_general(
        weighted, table[...], (((1,), (1,)), ((), ())),
        precision=HIGHEST, preferred_element_type=jnp.float32,
    )
    lane = lax.broadcasted_iota(jnp.int32, (16, width), 1)
    own = lax.rem(lax.broadcasted_iota(jnp.int32, (16, width), 0), 8)
    kept = jnp.full((16, width), -1, jnp.int32)
    for at in range(per_peer):
        kept = jnp.where(own == at, trunc_ref[me * per_peer + at], kept)
    keep = (lane % 8 == own) & (lane // 8 <= kept)
    filtered = jnp.dot(
        jnp.where(keep, spectrum, 0.0), table[...],
        precision=HIGHEST, preferred_element_type=jnp.float32,
    )
    for half in range(lat_devices):
        send2[half] = filtered[:, half * lat_local:(half + 1) * lat_local]
    for_peers(lambda offset: second(offset).start())
    recv2[me] = send2[lat]
    for_peers(lambda offset: second_arrival(offset).wait_recv())
    gathered = recv2[...].reshape(peers * 16, lat_local)
    out_ref[...] = jnp.dot(
        back[...], gathered, precision=HIGHEST, preferred_element_type=jnp.float32
    )
    for_peers(lambda offset: first(offset).wait_send())
    for_peers(lambda offset: second(offset).wait_send())


def spectral_forcing(cloud_state, truncation):
    lon_devices = lax.axis_size("lon")
    lat_devices = lax.axis_size("lat")
    peers = lon_devices * lat_devices
    _, lon_local, lat_local, cells = cloud_state.shape
    total_lon, total_lat = lon_local * lon_devices, lat_local * lat_devices
    modes = truncation.shape[0]
    chunks = 8 if lon_local % 8 == 0 else 1
    forward, back = wave_tables(total_lon, lon_devices, modes, peers, 1.0 / (total_lon * cells))
    lat_consts = latitude_rows(total_lat)
    starts = order_starts(modes, total_lat)
    vmem = pl.BlockSpec(memory_space=pltpu.VMEM)
    hbm = pl.BlockSpec(memory_space=pl.ANY)
    return pl.pallas_call(
        functools.partial(spectral_kernel, lon_devices, lat_devices, modes, chunks),
        out_shape=jax.ShapeDtypeStruct((lon_local, lat_local), jnp.float32),
        in_specs=[pl.BlockSpec(memory_space=pltpu.SMEM), hbm, hbm, hbm, vmem, vmem],
        out_specs=vmem,
        scratch_shapes=[
            pltpu.VMEM((lon_local, lat_local, cells), jnp.float32),
            pltpu.VMEM((NN * 8, total_lat), jnp.float32),
            pltpu.VMEM((lon_local, 8, lat_local), jnp.float32),
            pltpu.VMEM(forward.shape[1:], jnp.float32),
            pltpu.VMEM(back.shape[1:], jnp.float32),
            pltpu.VMEM((peers, 16, lat_local), jnp.float32),
            pltpu.VMEM((peers, 16, lat_local), jnp.float32),
            pltpu.VMEM((lat_devices, 16, lat_local), jnp.float32),
            pltpu.VMEM((peers, 16, lat_local), jnp.float32),
            pltpu.SemaphoreType.DMA((chunks,)),
            pltpu.SemaphoreType.DMA((2,)),
            pltpu.SemaphoreType.DMA((peers,)),
            pltpu.SemaphoreType.DMA((peers,)),
            pltpu.SemaphoreType.DMA((peers,)),
            pltpu.SemaphoreType.DMA((peers,)),
        ],
        compiler_params=pltpu.CompilerParams(
            collective_id=0, has_side_effects=True, vmem_limit_bytes=24 << 20
        ),
        name="spectral",
    )(truncation, cloud_state, jnp.asarray(forward), jnp.asarray(back), jnp.asarray(lat_consts), jnp.asarray(starts))


BATCH = 16


def swap_blocks(cols, low_half, even):
    a0 = jnp.where(low_half, cols[0], pltpu.roll(cols[2], 64, 1))
    b0 = jnp.where(low_half, pltpu.roll(cols[0], 64, 1), cols[2])
    a1 = jnp.where(low_half, cols[1], pltpu.roll(cols[3], 64, 1))
    b1 = jnp.where(low_half, pltpu.roll(cols[1], 64, 1), cols[3])
    return [
        jnp.where(even, a0, pltpu.roll(a1, 32, 1)),
        jnp.where(even, pltpu.roll(a0, 96, 1), a1),
        jnp.where(even, b0, pltpu.roll(b1, 32, 1)),
        jnp.where(even, pltpu.roll(b0, 96, 1), b1),
    ]


def cloud_kernel(lat_local, counts_ref, force_ref, const_ref, x_ref, o_ref):
    chunk = pl.program_id(0)
    blocks = x_ref.shape[1]
    rows = blocks * 8 // lat_local
    lane = lax.broadcasted_iota(jnp.int32, (8, 128), 1)
    low_half = lane < 64
    even = (lane // 32) % 2 == 0
    kappa = 0.275 / 0.725

    def batch(index, carry):
        spots = []
        for at in range(BATCH):
            column = index * BATCH + at
            row, lat = column // lat_local, column % lat_local
            spots.append((column // 8, column % 8, chunk * rows + row, lat))
        counts = [counts_ref[spot[2], spot[3]] for spot in spots]
        forces = [force_ref[spot[2], spot[3]] for spot in spots]
        most = functools.reduce(jnp.maximum, counts)
        rho = const_ref[0]
        profile = const_ref[1]
        us, ws, heats, trips = [], [], [], []
        for group in range(BATCH // 4):
            u4, w4 = [], []
            for at in range(group * 4, group * 4 + 4):
                block, sub = spots[at][0], spots[at][1]
                theta = x_ref[0, block, pl.ds(sub, 8, stride=8), :]
                moist = x_ref[1, block, pl.ds(sub, 8, stride=8), :]
                u4.append((10.0 / 0.725) * moist - (2.0 / 0.725) * theta - (10.0 / 0.725))
                w4.append(theta + 0.5 * moist)
            us += swap_blocks(u4, low_half, even)
            ws += swap_blocks(w4, low_half, even)

            def spread(values):
                first = jnp.where(even, values[0], values[1])
                second = jnp.where(even, values[2], values[3])
                return jnp.where(low_half, first, second)

            heats.append(spread(forces[group * 4:group * 4 + 4]) * profile)
            trips.append(spread(counts[group * 4:group * 4 + 4]))

        def advance(step, state):
            us, ws = state
            scale = const_ref[2 + 9 + step + 1]
            floor = scale * scale
            next_us, next_ws = [], []
            for group in range(BATCH // 4):
                active = step < trips[group]
                push = 2.0 * heats[group] * scale
                u4 = us[group * 4:group * 4 + 4]
                w4 = ws[group * 4:group * 4 + 4]
                u_before = [pltpu.roll(u4[3], 1, 0)] + list(u4[:3])
                w_before = [pltpu.roll(w4[3], 1, 0)] + list(w4[:3])
                for at in range(4):
                    y = u4[at] + rho * u_before[at] - push
                    z = y * y + floor
                    root = z * lax.rsqrt(z)
                    next_us.append(jnp.where(active, y - kappa * root, u4[at]))
                    next_ws.append(jnp.where(active, w4[at] + rho * w_before[at], w4[at]))
            return tuple(next_us), tuple(next_ws)

        us, ws = lax.fori_loop(0, most, advance, (tuple(us), tuple(ws)))

        for group in range(BATCH // 4):
            def spread_rows(base):
                rows4 = [const_ref[base + counts[group * 4 + at]] for at in range(4)]
                return jnp.where(
                    low_half, jnp.where(even, rows4[0], rows4[1]), jnp.where(even, rows4[2], rows4[3])
                )

            u_scale = spread_rows(2 + 18)
            w_scale = spread_rows(2)
            shift = trips[group].astype(jnp.float32) * heats[group] * (1.0 / 1.1) - 0.5 / 1.1
            u_theta = u_scale * (0.5 / 1.1)
            thetas, moists = [], []
            for at in range(4):
                u, w = us[group * 4 + at], ws[group * 4 + at]
                theta = w_scale * w - u_theta * u + shift
                thetas.append(theta)
                moists.append(u_scale * u + (1.0 + 0.2 * theta))
            thetas = swap_blocks(thetas, low_half, even)
            moists = swap_blocks(moists, low_half, even)
            for at in range(4):
                block, sub = spots[group * 4 + at][0], spots[group * 4 + at][1]
                o_ref[0, block, pl.ds(sub, 8, stride=8), :] = thetas[at]
                o_ref[1, block, pl.ds(sub, 8, stride=8), :] = moists[at]
        return carry

    lax.fori_loop(0, blocks * 8 // BATCH, batch, 0)


def cloud_constants(courant, levels):
    rate = jnp.tile(courant, 128 // levels)
    level = jnp.tile(jnp.sin(jnp.pi * (jnp.arange(levels).astype(jnp.float32) + 0.5) / levels), 128 // levels)
    keep = 1.0 - rate
    lower = 0.725 * keep
    inverse = 1.0 / lower

    def powers(base, first):
        out = [first]
        for _ in range(8):
            out.append(out[-1] * base)
        return out

    one = jnp.ones_like(rate)
    rows = [rate / keep, COUPLE * level]
    rows += powers(keep, one / 1.1) + powers(inverse, one) + powers(lower, one * 0.0725)
    return jnp.broadcast_to(jnp.stack(rows)[:, None, :], (len(rows), 8, 128))


def shards(cloud_state, counts, courant, truncation):
    fields, lon_local, lat_local, cells = cloud_state.shape
    levels = courant.shape[0]
    forcing = spectral_forcing(cloud_state, truncation)
    consts = cloud_constants(courant, levels)
    lat_blocks, tiles = lat_local // 8, cells // 128
    view = cloud_state.reshape(fields, lon_local, lat_blocks, 8, tiles, 128)
    view = view.transpose(0, 1, 2, 4, 3, 5).reshape(fields, lon_local * lat_blocks, tiles * 8, 128)
    rows = 4 if lon_local % 4 == 0 else 1
    block = pl.BlockSpec((fields, rows * lat_blocks, tiles * 8, 128), lambda i: (0, i, 0, 0))
    smem = pl.BlockSpec(memory_space=pltpu.SMEM)
    updated = pl.pallas_call(
        functools.partial(cloud_kernel, lat_local),
        out_shape=jax.ShapeDtypeStruct(view.shape, jnp.float32),
        grid=(lon_local // rows,),
        in_specs=[smem, smem, pl.BlockSpec(memory_space=pltpu.VMEM), block],
        out_specs=block,
        compiler_params=pltpu.CompilerParams(vmem_limit_bytes=24 << 20),
        name="cloud",
    )(counts, forcing, consts, view)
    updated = updated.reshape(fields, lon_local, lat_blocks, tiles, 8, 128).transpose(0, 1, 2, 4, 3, 5)
    return updated.reshape(cloud_state.shape)


def solution(mesh):
    return jax.shard_map(
        shards,
        mesh=mesh,
        in_specs=(P("grp", "lon", "lat", None), P(("grp", "lon"), "lat"), P(), P()),
        out_specs=P("grp", "lon", "lat", None),
        check_vma=False,
    )
```

profile of v0, /device:TPU:4, one launch (start us, length us, event | category | flops | bytes accessed | tf_op | source)
XLA Modules:
  0.0 148.2 jit_solution(6541573892725640027)
XLA Ops:
  0.0 0.0 copy-start.5
  0.1 0.1 mul.554
  0.1 0.7 tile.6
  0.8 0.1 tile.7
  1.0 0.1 stack.8
  1.1 0.0 copy-start
  1.1 5.8 %copy-done = f32[2,32,64,1024]{3,2,1,0:T(8,128)S(1)} copy-done((f32[2,32,64,1024]{3,2,1,0:T(8,128)S(1)}, f32[2,32,64,1024]{3,2,1,0:T(8,128)}, u32[]{:S(2)}) %copy-start) | copy-done | bytes 16777240
  6.8 0.0 copy-start.2
  6.8 1.2 copy-done.2
  8.1 0.0 copy-start.3
  8.1 0.9 copy-done.3
  9.0 0.0 copy-start.4
  9.0 0.8 copy-done.4
  9.8 0.0 copy-start.6
  9.8 0.7 copy-done.6
  10.5 0.0 copy-start.7
  10.5 0.7 copy-done.7
  11.2 0.0 copy-start.1
  11.2 21.2 %spectral.1.force_ref = f32[32,64]{1,0:T(8,128)S(1)} custom-call(s32[96]{0:T(128)S(1)} %copy-done.7, f32[2,32,64,1024]{3,2,1,0:T(8,128)S(1)} %copy-done, f32[8,256,32]{2,1,0:T(8,128)S(1)} %copy-done.2, f32[8,32,256]{2,1,0:T(8,128)S(1)} %copy-done.3, f32[3,8,128]{2,1,0:T(8,128)S(1)} %copy-done.6, f32[104,128]{1,0:T(8,128)S(1)} %copy-done.4), custom_call_target="tpu_custom_call" | custom-call | tf_op jit(solution)/shard_map/spectral/pallas_call | solution.py:230
  32.4 0.0 copy-done.5
  32.4 0.0 copy-done.1
  32.4 115.7 %cloud.1 = f32[2,256,64,128]{3,2,1,0:T(8,128)} custom-call(s32[32,64]{1,0:T(8,128)S(1)} %copy-done.5, f32[32,64]{1,0:T(8,128)S(1)} %spectral.1.force_ref, f32[29,8,128]{2,1,0:T(8,128)S(1)} %broadcast_in_dim.2.const_ref, f32[2,256,64,128]{3,2,1,0:T(8,128)S(1)} %bitcast.10), custom_call_target="tpu_custom_call" | custom-call | tf_op jit(solution)/shard_map/cloud/pallas_call | solution.py:395
  (9 shorter events, 0.1 us)
Async XLA Ops:
  0.0 32.4 %copy-start.5 = (s32[32,64]{1,0:T(8,128)S(1)}, s32[32,64]{1,0:T(8,128)}, u32[]{:S(2)}) copy-start(s32[32,64]{1,0:T(8,128)} %counts_ref.1) | copy-start | bytes 24580
  1.1 5.8 %copy-start = (f32[2,32,64,1024]{3,2,1,0:T(8,128)S(1)}, f32[2,32,64,1024]{3,2,1,0:T(8,128)}, u32[]{:S(2)}) copy-start(f32[2,32,64,1024]{3,2,1,0:T(8,128)} %state_ref.1) | copy-start | bytes 50331652
  6.8 1.2 copy-start.2
  8.1 0.9 copy-start.3
  9.0 0.8 copy-start.4
  9.8 0.7 copy-start.6
  10.5 0.7 copy-start.7
  11.2 21.3 %copy-start.1 = (f32[2,32,64,1024]{3,2,1,0:T(8,128)S(1)}, f32[2,32,64,1024]{3,2,1,0:T(8,128)}, u32[]{:S(2)}) copy-start(f32[2,32,64,1024]{3,2,1,0:T(8,128)} %state_ref.1) | copy-start | bytes 50331652
where the time goes:
time: 148 us
  Pallas kernels  137 us (93%)
  local copies, waits for them, and re-layouts  11.1 us (8%)
    pallas_call x1, Pallas kernels, shards(): pl.pallas_call(functools.partial(cloud_kernel, lat_local), out_shape=jax....  116 us
    pallas_call x1, Pallas kernels, spectral_forcing(): pl.pallas_call(functools.partial(spectral_kernel, lon_devices, lat_device...  21.2 us
    unnamed x16, local copies, waits for them, and re-layouts  10.1 us

commit v1 on v0

--- a/solution.py
+++ b/solution.py
@@ -44,10 +44,61 @@
     return np.repeat((0.5 * np.log(0.5) + gains)[:, None], total_lat, axis=1).astype(np.float32)
 
 
+def order_columns(counts_ref, order_ref, ranks, batch_rows):
+    lon_local, lat_local = counts_ref.shape
+    groups, batch = order_ref.shape[1:]
+    narrow = jnp.bfloat16
+
+    def product(a, b):
+        return jnp.dot(a, b.astype(narrow), preferred_element_type=jnp.float32)
+
+    counts = counts_ref[...]
+    at_row = lax.broadcasted_iota(jnp.int32, (lat_local, lat_local), 0)
+    at_col = lax.broadcasted_iota(jnp.int32, (lat_local, lat_local), 1)
+    before = (at_row < at_col).astype(jnp.float32)
+    every = jnp.ones((lat_local, lat_local), jnp.float32)
+    row = lax.broadcasted_iota(jnp.int32, (lon_local, lon_local), 0)
+    col = lax.broadcasted_iota(jnp.int32, (lon_local, lon_local), 1)
+    same = row // batch_rows == col // batch_rows
+    above = (same & (col < row)).astype(jnp.float32).astype(narrow)
+    block = same.astype(jnp.float32).astype(narrow)
+    rank = jnp.zeros((lon_local, lat_local), jnp.float32)
+    fewer = jnp.zeros((lon_local, lat_local), jnp.float32)
+    for value in range(1, 9):
+        member = (counts == value).astype(jnp.float32)
+        in_row = product(member.astype(narrow), before)
+        row_sums = product(member.astype(narrow), every)
+        rank = rank + member * (fewer + in_row + product(above, row_sums))
+        fewer = fewer + product(block, row_sums)
+    ranks[...] = rank.astype(jnp.int32)
+
+    spot = lax.broadcasted_iota(jnp.int32, (groups, lat_local), 0)
+    slot = lax.broadcasted_iota(jnp.int32, (batch, lat_local), 0)
+    lats = lax.broadcasted_iota(jnp.int32, (batch, lat_local), 1)
+
+    def invert(chunk, carry):
+        columns = jnp.zeros((groups, batch), jnp.float32)
+        amounts = jnp.zeros((groups, batch), jnp.float32)
+        for at in range(batch_rows):
+            line = pl.ds(chunk * batch_rows + at, 1)
+            mine = ranks[line, :]
+            high = (spot == mine // batch).astype(jnp.float32).astype(narrow)
+            low = slot == mine % batch
+            column = jnp.where(low, lats + at * lat_local, 0).astype(jnp.float32).astype(narrow)
+            amount = jnp.where(low, counts_ref[line, :], 0).astype(jnp.float32).astype(narrow)
+            dims = (((1,), (1,)), ((), ()))
+            columns += lax.dot_general(high, column, dims, preferred_element_type=jnp.float32)
+            amounts += lax.dot_general(high, amount, dims, preferred_element_type=jnp.float32)
+        order_ref[chunk] = (columns + 256.0 * amounts).astype(jnp.int32)
+        return carry
+
+    lax.fori_loop(0, order_ref.shape[0], invert, 0)
+
+
 def spectral_kernel(
-    lon_devices, lat_devices, modes, chunks,
-    trunc_ref, state_ref, forward_ref, back_ref, lat_ref, start_ref, out_ref,
-    theta, table, heat, forward, back, send1, recv1, send2, recv2,
+    lon_devices, lat_devices, modes, chunks, batch_rows,
+    trunc_ref, state_ref, forward_ref, back_ref, lat_ref, counts_ref, out_ref, order_ref,
+    theta, table, heat, ranks, forward, back, send1, recv1, send2, recv2,
     load_sem, table_sem, s1_sem, r1_sem, s2_sem, r2_sem,
 ):
     grp = lax.axis_index("grp")
@@ -84,13 +135,13 @@
     lax.fori_loop(1, peers, greet, 0)
 
     total_lat = table.shape[1]
-    sin_lat = lat_ref[0]
-    weight = lat_ref[1]
+    sin_lat = lat_ref[0:8]
+    weight = lat_ref[8:16]
     order_f = (me * per_peer + lax.broadcasted_iota(jnp.int32, (8, total_lat), 0)).astype(jnp.float32)
     start = jnp.concatenate(
-        [start_ref[pl.ds(me * per_peer + at, 1), :] for at in range(8)], axis=0
-    )
-    diagonal = jnp.exp(start + order_f * lat_ref[2])
+        [lat_ref[pl.ds(24 + me * per_peer + at, 1), :] for at in range(8)], axis=0
+    )
+    diagonal = jnp.exp(start + order_f * lat_ref[16:24])
     zero = jnp.zeros((8, total_lat), jnp.float32)
 
     def rung(degree_f, carry):
@@ -98,8 +149,9 @@
         higher = degree_f > order_f
         numerator = jnp.maximum(4.0 * degree_f * degree_f - 1.0, 1.0)
         denominator = jnp.where(higher, degree_f * degree_f - order_f * order_f, 1.0)
-        factor = jnp.sqrt(numerator / denominator)
-        back_factor = jnp.sqrt(denominator / numerator)
+        mixed = lax.rsqrt(numerator * denominator)
+        factor = numerator * mixed
+        back_factor = denominator * mixed
         raised = factor * (sin_lat * previous - inverse * earlier)
         current = jnp.where(degree_f == order_f, diagonal, jnp.where(higher, raised, 0.0))
         return current, previous, jnp.where(higher, back_factor, 0.0)
@@ -116,22 +168,23 @@
     ones = jnp.ones((8, 128), jnp.float32)
     for chunk in range(chunks):
         theta_copy(chunk).wait()
-
-        def add_row(at, carry):
+        totals = []
+        for at in range(rows):
             row = chunk * rows + at
             total = theta[row, :, 0:128]
             for tile in range(1, cells // 128):
                 total = total + theta[row, :, tile * 128:(tile + 1) * 128]
-            heat[row] = lax.dot_general(
-                ones, total, (((1,), (1,)), ((), ())),
-                precision=HIGHEST, preferred_element_type=jnp.float32,
-            )
-            return carry
-
-        lax.fori_loop(0, rows, add_row, 0)
+            totals.append(total)
+        sums = lax.dot_general(
+            ones, jnp.concatenate(totals, axis=0), (((1,), (1,)), ((), ())),
+            precision=HIGHEST, preferred_element_type=jnp.float32,
+        )
+        for at in range(rows):
+            row = chunk * rows + at
+            heat[row:row + 1, :] = sums[0:1, at * lat_local:(at + 1) * lat_local]
     forward_copy.wait()
     back_copy.wait()
-    heating = heat[:, 0, :]
+    heating = heat[...]
     coefs = jnp.dot(forward[...], heating, precision=HIGHEST, preferred_element_type=jnp.float32)
     send1[...] = coefs.reshape(peers, 16, lat_local)
     pl.semaphore_wait(barrier, peers - 1)
@@ -176,6 +229,7 @@
 
     for_peers(lambda offset: first(offset).start())
     recv1[me] = send1[me]
+    order_columns(counts_ref, order_ref, ranks, batch_rows)
     for_peers(lambda offset: first_arrival(offset).wait_recv())
     halves = []
     for half in range(lat_devices):
@@ -214,7 +268,7 @@
     for_peers(lambda offset: second(offset).wait_send())
 
 
-def spectral_forcing(cloud_state, truncation):
+def spectral_forcing(cloud_state, counts, truncation, batch_rows):
     lon_devices = lax.axis_size("lon")
     lat_devices = lax.axis_size("lat")
     peers = lon_devices * lat_devices
@@ -223,19 +277,25 @@
     modes = truncation.shape[0]
     chunks = 8 if lon_local % 8 == 0 else 1
     forward, back = wave_tables(total_lon, lon_devices, modes, peers, 1.0 / (total_lon * cells))
-    lat_consts = latitude_rows(total_lat)
-    starts = order_starts(modes, total_lat)
+    lat_consts = np.concatenate(
+        [latitude_rows(total_lat).reshape(24, total_lat), order_starts(modes, total_lat)]
+    )
+    groups = batch_rows * lat_local // BATCH
     vmem = pl.BlockSpec(memory_space=pltpu.VMEM)
     hbm = pl.BlockSpec(memory_space=pl.ANY)
     return pl.pallas_call(
-        functools.partial(spectral_kernel, lon_devices, lat_devices, modes, chunks),
-        out_shape=jax.ShapeDtypeStruct((lon_local, lat_local), jnp.float32),
+        functools.partial(spectral_kernel, lon_devices, lat_devices, modes, chunks, batch_rows),
+        out_shape=(
+            jax.ShapeDtypeStruct((lon_local, lat_local), jnp.float32),
+            jax.ShapeDtypeStruct((lon_local // batch_rows, groups, BATCH), jnp.int32),
+        ),
         in_specs=[pl.BlockSpec(memory_space=pltpu.SMEM), hbm, hbm, hbm, vmem, vmem],
-        out_specs=vmem,
+        out_specs=(vmem, vmem),
         scratch_shapes=[
             pltpu.VMEM((lon_local, lat_local, cells), jnp.float32),
             pltpu.VMEM((NN * 8, total_lat), jnp.float32),
-            pltpu.VMEM((lon_local, 8, lat_local), jnp.float32),
+            pltpu.VMEM((lon_local, lat_local), jnp.float32),
+            pltpu.VMEM((lon_local, lat_local), jnp.int32),
             pltpu.VMEM(forward.shape[1:], jnp.float32),
             pltpu.VMEM(back.shape[1:], jnp.float32),
             pltpu.VMEM((peers, 16, lat_local), jnp.float32),
@@ -250,10 +310,10 @@
             pltpu.SemaphoreType.DMA((peers,)),
         ],
         compiler_params=pltpu.CompilerParams(
-            collective_id=0, has_side_effects=True, vmem_limit_bytes=24 << 20
+            collective_id=0, has_side_effects=True, vmem_limit_bytes=60 << 20
         ),
         name="spectral",
-    )(truncation, cloud_state, jnp.asarray(forward), jnp.asarray(back), jnp.asarray(lat_consts), jnp.asarray(starts))
+    )(truncation, cloud_state, jnp.asarray(forward), jnp.asarray(back), jnp.asarray(lat_consts), counts)
 
 
 BATCH = 16
@@ -272,7 +332,7 @@
     ]
 
 
-def cloud_kernel(lat_local, counts_ref, force_ref, const_ref, x_ref, o_ref):
+def cloud_kernel(lat_local, order_ref, force_ref, const_ref, x_ref, o_ref):
     chunk = pl.program_id(0)
     blocks = x_ref.shape[1]
     rows = blocks * 8 // lat_local
@@ -280,16 +340,16 @@
     low_half = lane < 64
     even = (lane // 32) % 2 == 0
     kappa = 0.275 / 0.725
+    lat_bits = lat_local.bit_length() - 1
 
     def batch(index, carry):
-        spots = []
-        for at in range(BATCH):
-            column = index * BATCH + at
-            row, lat = column // lat_local, column % lat_local
-            spots.append((column // 8, column % 8, chunk * rows + row, lat))
-        counts = [counts_ref[spot[2], spot[3]] for spot in spots]
-        forces = [force_ref[spot[2], spot[3]] for spot in spots]
-        most = functools.reduce(jnp.maximum, counts)
+        entries = [order_ref[chunk, index, at] for at in range(BATCH)]
+        spots = [((entry & 255) >> 3, entry & 7) for entry in entries]
+        counts = [entry >> 8 for entry in entries]
+        forces = [
+            force_ref[chunk * rows + ((entry & 255) >> lat_bits), entry & (lat_local - 1)]
+            for entry in entries
+        ]
         rho = const_ref[0]
         profile = const_ref[1]
         us, ws, heats, trips = [], [], [], []
@@ -312,7 +372,7 @@
             heats.append(spread(forces[group * 4:group * 4 + 4]) * profile)
             trips.append(spread(counts[group * 4:group * 4 + 4]))
 
-        def advance(step, state):
+        def advance(masked, step, state):
             us, ws = state
             scale = const_ref[2 + 9 + step + 1]
             floor = scale * scale
@@ -328,11 +388,16 @@
                     y = u4[at] + rho * u_before[at] - push
                     z = y * y + floor
                     root = z * lax.rsqrt(z)
-                    next_us.append(jnp.where(active, y - kappa * root, u4[at]))
-                    next_ws.append(jnp.where(active, w4[at] + rho * w_before[at], w4[at]))
+                    next_us.append(y - kappa * root)
+                    next_ws.append(w4[at] + rho * w_before[at])
+                    if masked:
+                        next_us[-1] = jnp.where(active, next_us[-1], u4[at])
+                        next_ws[-1] = jnp.where(active, next_ws[-1], w4[at])
             return tuple(next_us), tuple(next_ws)
 
-        us, ws = lax.fori_loop(0, most, advance, (tuple(us), tuple(ws)))
+        state = (tuple(us), tuple(ws))
+        state = lax.fori_loop(0, counts[0], functools.partial(advance, False), state)
+        us, ws = lax.fori_loop(counts[0], counts[-1], functools.partial(advance, True), state)
 
         for group in range(BATCH // 4):
             def spread_rows(base):
@@ -384,12 +449,12 @@
 def shards(cloud_state, counts, courant, truncation):
     fields, lon_local, lat_local, cells = cloud_state.shape
     levels = courant.shape[0]
-    forcing = spectral_forcing(cloud_state, truncation)
+    rows = min(256 // lat_local, lon_local)
+    forcing, order = spectral_forcing(cloud_state, counts, truncation, rows)
     consts = cloud_constants(courant, levels)
     lat_blocks, tiles = lat_local // 8, cells // 128
     view = cloud_state.reshape(fields, lon_local, lat_blocks, 8, tiles, 128)
     view = view.transpose(0, 1, 2, 4, 3, 5).reshape(fields, lon_local * lat_blocks, tiles * 8, 128)
-    rows = 4 if lon_local % 4 == 0 else 1
     block = pl.BlockSpec((fields, rows * lat_blocks, tiles * 8, 128), lambda i: (0, i, 0, 0))
     smem = pl.BlockSpec(memory_space=pltpu.SMEM)
     updated = pl.pallas_call(
@@ -398,9 +463,9 @@
         grid=(lon_local // rows,),
         in_specs=[smem, smem, pl.BlockSpec(memory_space=pltpu.VMEM), block],
         out_specs=block,
-        compiler_params=pltpu.CompilerParams(vmem_limit_bytes=24 << 20),
+        compiler_params=pltpu.CompilerParams(vmem_limit_bytes=60 << 20),
         name="cloud",
-    )(counts, forcing, consts, view)
+    )(order, forcing, consts, view)
     updated = updated.reshape(fields, lon_local, lat_blocks, tiles, 8, 128).transpose(0, 1, 2, 4, 3, 5)
     return updated.reshape(cloud_state.shape)
 

time: 148 us -> 111 us (0.75)
  the two profiles are of different devices: /device:TPU:4 before, /device:TPU:2 now
where the time goes in v1:
time: 111 us; the launch traced here: 110 us
  Pallas kernels  108 us (97%)
  local copies, waits for them, and re-layouts  1.58 us (1%)
    pallas_call x1, Pallas kernels, shards(): pl.pallas_call(functools.partial(cloud_kernel, lat_local), out_shape=jax....  89.6 us
    pallas_call x1, Pallas kernels, spectral_forcing(): pl.pallas_call(functools.partial(spectral_kernel, lon_devices, lat_device...  18.8 us

profile of v1, /device:TPU:2, one launch (start us, length us, event | category | flops | bytes accessed | tf_op | source)
XLA Modules:
  0.0 110.1 jit_solution(16432592274378858339)
XLA Ops:
  0.1 0.1 mul.554
  0.1 0.7 tile.6
  0.8 0.1 tile.7
  1.0 0.1 stack.8
  1.1 18.8 %spectral.1 = (f32[32,64]{1,0:T(8,128)}, s32[8,16,16]{2,1,0:T(8,128)}) custom-call(s32[96]{0:T(128)} %trunc_ref.1, f32[2,32,64,1024]{3,2,1,0:T(8,128)} %state_ref.1, f32[8,256,32]{2,1,0:T(8,128)} %constant.28.clone.forward_ref, f32[8,32,256]{2,1,0:T(8,128)} %constant.29.clone.back_ref, f32[128,128]{1,0:T(8,128)} %constant.30.clone.lat_ref, s32[32,64]{1,0:T(8,128)} %counts_ref.1), custom_call_target="tpu_custom_call" | custom-call | tf_op jit(solution)/shard_map/spectral/pallas_call | solution.py:286
  19.9 0.7 broadcast_in_dim.2.const_ref
  20.6 89.6 %cloud.1 = f32[2,256,64,128]{3,2,1,0:T(8,128)} custom-call(s32[8,16,16]{2,1,0:T(8,128)} %get-tuple-element.7.order_ref, f32[32,64]{1,0:T(8,128)} %get-tuple-element.8.force_ref, f32[29,8,128]{2,1,0:T(8,128)} %broadcast_in_dim.2.const_ref, f32[2,256,64,128]{3,2,1,0:T(8,128)} %bitcast.10), custom_call_target="tpu_custom_call" | custom-call | tf_op jit(solution)/shard_map/cloud/pallas_call | solution.py:460
  (8 shorter events, 0.1 us)
